TPU v7x, 512 devices: a whole 4x8x8 slice. The times are simulated.
512 devices in a mesh: occ: 16 (over y, core), vir: 32 (over x, z).
Axes of the slice: x: 4, y: 8, z: 8, core: 2. Of those that a mesh axis runs over, the one named last changes fastest.
Arguments:
- amplitudes: float32 [2048, 12288], P('occ', 'vir'), may hold values from -6 to 6
- integrals: float32 [12288, 4096], P('vir', 'occ'), may hold values from -0.109375 to 0.109375
- pair_mask: int32 [32, 192], P('occ', 'vir'), may hold values 0 or 1
- tile_mask: int32 [192, 64], P('vir', 'occ'), may hold values 0 or 1
Outputs:
- residual: float32 [2048, 4096], P('occ', 'vir')
Inputs may be any that keep to these rules, and one draw needn't show every extreme that they name: `pair_mask`: 0 marks a tile that is absent and contributes nothing. `tile_mask`: 0 marks a tile that is absent and contributes nothing.
All inputs are finite; a program needn't handle non-finite values. No bound on the sum of `pair_mask` or of `tile_mask` on one device may be relied on, other than what follows from the above.
Results may differ from a plain program's by a relative error of at most 0.00007.
Values sent between devices are 32-bit elements; how exact they have to be, the bound alone decides.
No kernel may reach another device: no remote copies, remote signals or barrier semaphores. Data moves between devices by JAX's collectives and lax.ppermute only.
A program may use at most 64 MiB of HBM per device.

v0:
```python
import jax
import jax.numpy as jnp
from jax import lax
from jax.sharding import Mesh, PartitionSpec as P

AXES = ("h", "l", "c", "x", "z")
SIZES = (4, 2, 2, 4, 8)


def moves(names, target):
    sizes = [SIZES[AXES.index(name)] for name in names]
    pairs = []
    total = 1
    for size in sizes:
        total *= size
    for source in range(total):
        rest, at = (source, {})
        for name, size in zip(names[::-1], sizes[::-1]):
            at[name], rest = (rest % size, rest // size)
        to = dict(at, **target(at))
        index = 0
        for name, size in zip(names, sizes):
            index = index * size + to[name] % size
        pairs.append((source, index))
    return pairs


def send(value, names, target):
    return lax.ppermute(value, names, moves(names, target))


def expand(mask, width):
    grown = jnp.repeat(mask.astype(jnp.float32), width, axis=0)
    return jnp.repeat(grown, width, axis=1)


def product(a, b):
    return jnp.dot(a, b, precision=lax.Precision.HIGH, preferred_element_type=jnp.float32)


def sign(at):
    return 1 - 2 * ((at["x"] + at["c"]) % 2)


def body(amplitudes, integrals, pair_mask, tile_mask):
    l = lax.axis_index("l")
    width = amplitudes.shape[1] // pair_mask.shape[1]
    masked_v = integrals * expand(tile_mask, width)
    far_half = send(masked_v, ("l",), lambda at: {"l": at["l"] + 1})
    near = lax.all_gather(masked_v, "c", axis=1, tiled=True)
    near_beside = send(near, ("c", "x"), lambda at: {"x": at["x"] + sign(at)})
    masked_t = amplitudes * expand(pair_mask, width)
    names = ("h", "c", "x")
    own = jnp.concatenate(
        [
            send(masked_t, names, lambda at: {"h": at["h"] - at["x"]}),
            send(masked_t, names, lambda at: {"h": at["h"] - at["x"] + sign(at)}),
        ]
    )
    beside = jnp.concatenate(
        [
            send(
                masked_t,
                names,
                lambda at: {"h": at["h"] - at["x"] - sign(at), "x": at["x"] + sign(at)},
            ),
            send(
                masked_t,
                names,
                lambda at: {"h": at["h"] - at["x"] - 2 * sign(at), "x": at["x"] + sign(at)},
            ),
        ]
    )
    far = lax.all_gather(far_half, "c", axis=1, tiled=True)
    far_beside = send(far, ("c", "x"), lambda at: {"x": at["x"] + sign(at)})
    near_sum = product(own, near) + product(beside, near_beside)
    far_sum = product(own, far) + product(beside, far_beside)
    away = jnp.concatenate([near_sum[128:], far_sum[128:]], axis=1)
    came = send(away, ("c", "x"), lambda at: {"x": at["x"] - sign(at)})
    near_sum, far_sum = (near_sum[:128] + came[:, :512], far_sum[:128] + came[:, 512:])
    low = l == 0
    halves = jnp.concatenate(
        [jnp.where(low, near_sum, far_sum), jnp.where(low, far_sum, near_sum)], axis=1
    )
    pieces = halves.reshape(128, 8, 128).transpose(1, 0, 2)
    groups = []
    for first in range(0, 512, 8):
        core = first // 32 % 2
        groups.append([first + (k + 4 * core) % 8 for k in range(8)])
    turn = lax.axis_index("c") * 4
    pieces = jnp.concatenate([pieces, pieces[:4]])
    pieces = lax.dynamic_slice_in_dim(pieces, turn, 8, 0)
    total = lax.all_to_all(pieces, AXES, 0, 0, tiled=True, axis_index_groups=groups).sum(0)
    return send(total, ("h", "x"), lambda at: {"h": at["h"] + at["x"], "x": at["h"]})


def solution(mesh):
    fine = Mesh(mesh.devices.reshape(SIZES), AXES)
    occ, vir = (("h", "l", "c"), ("x", "z"))
    in_specs = (P(occ, vir), P(vir, occ), P(occ, vir), P(vir, occ))
    return jax.shard_map(body, mesh=fine, in_specs=in_specs, out_specs=P(occ, vir), check_vma=False)
```

profile of v0, /device:TPU:40, one launch (start us, length us, event | category | flops | bytes accessed | tf_op | source)
XLA Modules:
  0.0 96.9 jit_solution(14063444466938659748)
XLA Ops:
  0.0 1.1 %copy.13 = f32[128,384]{0,1:T(8,128)S(1)} copy(f32[128,384]{1,0:T(8,128)} %param.4) | data formatting | bytes 393216 | tf_op args[0]
  1.1 0.1 copy.12
  1.2 0.1 broadcast_in_dim.12
  1.3 0.1 reshape.15
  1.4 4.1 %collective-permute-start.2 = (f32[128,384]{0,1:T(8,128)S(1)}, f32[128,384]{0,1:T(8,128)S(1)}, u32[]{:S(2)}, u32[]{:S(2)}) collective-permute-start(f32[128,384]{0,1:T(8,128)S(1)} %bitcast_multiply_fusion.1), channel_id=1, source_target_pairs={{0,392},{8,0},{16,152},{24,272},{32,184},{40,304},{48,424},{56,32}... | collective-permute-start | bytes 589832 | tf_op jit(solution)/shard_map/ppermute | solution.py:29
  5.5 0.2 copy.14
  5.7 0.1 broadcast_in_dim.14
  5.8 0.1 reshape.17
  5.9 2.4 %collective-permute-start.5 = (f32[384,256]{0,1:T(8,128)S(1)}, f32[384,256]{0,1:T(8,128)S(1)}, u32[]{:S(2)}, u32[]{:S(2)}) collective-permute-start(f32[384,256]{0,1:T(8,128)S(1)} %bitcast_multiply_fusion), channel_id=1, source_target_pairs={{0,64},{64,0},{1,65},{65,1},{2,66},{66,2},{3,67},{67,3},{4,68},{68... | collective-permute-start | bytes 1179656 | tf_op jit(solution)/shard_map/ppermute | solution.py:29
  8.3 3.0 %all_gather.6 = f32[384,512]{0,1:T(8,128)S(1)} all-gather(f32[384,256]{0,1:T(8,128)S(1)} %bitcast_multiply_fusion), channel_id=1, replica_groups=mesh['h'=4,'l'=2,'c'=2,'x'=4,'z'=8] {'c'}, dimensions={1}, use_global_device_ids=true | all-gather | bytes 1179648 | tf_op jit(solution)/shard_map/all_gather | solution.py:50
  11.2 2.0 %collective-permute-start.4 = (f32[384,512]{0,1:T(8,128)S(1)}, f32[384,512]{0,1:T(8,128)S(1)}, u32[]{:S(2)}, u32[]{:S(2)}) collective-permute-start(f32[384,512]{0,1:T(8,128)S(1)} %all_gather.6), channel_id=1, source_target_pairs={{0,8},{8,0},{16,24},{24,16},{32,56},{40,48},{48,40},{56,32},{1,9},... | collective-permute-start | bytes 2359304 | tf_op jit(solution)/shard_map/ppermute | solution.py:29
  13.3 6.8 %collective-permute-start.3 = (f32[128,384]{0,1:T(8,128)S(1)}, f32[128,384]{0,1:T(8,128)S(1)}, u32[]{:S(2)}, u32[]{:S(2)}) collective-permute-start(f32[128,384]{0,1:T(8,128)S(1)} %bitcast_multiply_fusion.1), channel_id=1, source_target_pairs={{0,264},{8,128},{16,24},{24,400},{32,312},{40,176},{48,40},{56,416... | collective-permute-start | bytes 589832 | tf_op jit(solution)/shard_map/ppermute | solution.py:29
  20.1 0.7 collective-permute-start
  20.8 4.0 %collective-permute-start.1 = (f32[128,384]{0,1:T(8,128)S(1)}, f32[128,384]{0,1:T(8,128)S(1)}, u32[]{:S(2)}, u32[]{:S(2)}) collective-permute-start(f32[128,384]{0,1:T(8,128)S(1)} %bitcast_multiply_fusion.1), channel_id=1, source_target_pairs={{0,128},{8,264},{16,400},{24,24},{32,416},{40,40},{48,176},{56,312... | collective-permute-start | bytes 589832 | tf_op jit(solution)/shard_map/ppermute | solution.py:29
  24.9 2.4 %all_gather.7 = f32[384,512]{0,1:T(8,128)S(1)} all-gather(f32[384,256]{0,1:T(8,128)S(1)} %collective-permute-done.5), channel_id=1, replica_groups=mesh['h'=4,'l'=2,'c'=2,'x'=4,'z'=8] {'c'}, dimensions={1}, use_global_device_ids=true | all-gather | bytes 1179648 | tf_op jit(solution)/shard_map/all_gather | solution.py:74
  27.2 7.2 %collective-permute-start.6 = (f32[384,512]{0,1:T(8,128)S(1)}, f32[384,512]{0,1:T(8,128)S(1)}, u32[]{:S(2)}, u32[]{:S(2)}) collective-permute-start(f32[384,512]{0,1:T(8,128)S(1)} %all_gather.7), channel_id=1, source_target_pairs={{0,8},{8,0},{16,24},{24,16},{32,56},{40,48},{48,40},{56,32},{1,9},... | collective-permute-start | bytes 2359304 | tf_op jit(solution)/shard_map/ppermute | solution.py:29
  34.5 1.8 %collective-permute-done.1 = f32[128,384]{0,1:T(8,128)S(1)} collective-permute-done((f32[128,384]{0,1:T(8,128)S(1)}, f32[128,384]{0,1:T(8,128)S(1)}, u32[]{:S(2)}, u32[]{:S(2)}) %collective-permute-start.1) | collective-permute-done | bytes 196640 | tf_op jit(solution)/shard_map/ppermute | solution.py:29
  36.4 0.9 fusion.1
  37.3 0.9 convolution_add_fusion.1
  38.1 0.8 copy-done
  38.9 5.5 %collective-permute-done.6 = f32[384,512]{0,1:T(8,128)S(1)} collective-permute-done((f32[384,512]{0,1:T(8,128)S(1)}, f32[384,512]{0,1:T(8,128)S(1)}, u32[]{:S(2)}, u32[]{:S(2)}) %collective-permute-start.6) | collective-permute-done | bytes 786464 | tf_op jit(solution)/shard_map/ppermute | solution.py:29
  44.4 0.9 fusion.2
  45.3 0.9 convolution_add_fusion
  46.2 0.9 slice-done
  47.1 4.1 %collective-permute-start.7 = (f32[128,1024]{1,0:T(8,128)S(1)}, f32[128,1024]{1,0:T(8,128)S(1)}, u32[]{:S(2)}, u32[]{:S(2)}) collective-permute-start(f32[128,1024]{1,0:T(8,128)S(1)} %pad_maximum_fusion), channel_id=1, source_target_pairs={{0,24},{8,16},{16,8},{24,0},{32,40},{40,32},{48,56},{56,48},{1,25}... | collective-permute-start | bytes 1572872 | tf_op jit(solution)/shard_map/ppermute | solution.py:29
  51.3 8.3 %collective-permute-done.7 = f32[128,1024]{1,0:T(8,128)S(1)} collective-permute-done((f32[128,1024]{1,0:T(8,128)S(1)}, f32[128,1024]{1,0:T(8,128)S(1)}, u32[]{:S(2)}, u32[]{:S(2)}) %collective-permute-start.7) | collective-permute-done | bytes 524320 | tf_op jit(solution)/shard_map/ppermute | solution.py:29
  59.6 0.1 broadcast_select_fusion.1
  59.7 0.1 fusion
  59.8 23.2 %all_to_all.5 = f32[8,128,128]{2,1,0:T(8,128)S(1)} all-to-all(f32[8,128,128]{2,1,0:T(8,128)S(1)} %fusion), channel_id=1, replica_groups={{0,1,2,3,4,5,6,7},{8,9,10,11,12,13,14,15},{16,17,18,19,20,21,22,23},{24..., dimensions={0} | all-to-all | bytes 1048576 | tf_op jit(solution)/shard_map/all_to_all | solution.py:93
  83.0 4.6 %collective-permute-start.8 = (f32[128,128]{1,0:T(8,128)S(1)}, f32[128,128]{1,0:T(8,128)S(1)}, u32[]{:S(2)}, u32[]{:S(2)}) collective-permute-start(f32[128,128]{1,0:T(8,128)S(1)} %reduce_sum.9), channel_id=1, source_target_pairs={{0,0},{8,128},{16,256},{24,384},{128,136},{136,264},{144,392},{152... | collective-permute-start | bytes 196616 | tf_op jit(solution)/shard_map/ppermute | solution.py:29
  87.6 8.6 %collective-permute-done.8 = f32[128,128]{1,0:T(8,128)S(1)} collective-permute-done((f32[128,128]{1,0:T(8,128)S(1)}, f32[128,128]{1,0:T(8,128)S(1)}, u32[]{:S(2)}, u32[]{:S(2)}) %collective-permute-start.8) | collective-permute-done | bytes 65568 | tf_op jit(solution)/shard_map/ppermute | solution.py:29
  96.2 0.6 copy.21
  (28 shorter events, 0.3 us)
Async XLA Ops:
  0.0 1.1 %copy-start.4 = (s32[2,6]{1,0:T(2,128)S(1)}, s32[2,6]{1,0:T(2,128)}, u32[]{:S(2)}) copy-start(s32[2,6]{1,0:T(2,128)} %param.6) | copy-start | bytes 148
  0.0 5.5 %copy-start.2 = (f32[384,256]{1,0:T(8,128)S(1)}, f32[384,256]{1,0:T(8,128)}, u32[]{:S(2)}) copy-start(f32[384,256]{1,0:T(8,128)} %param.5) | copy-start | bytes 1179652
  1.4 4.3 %copy-start.3 = (s32[6,4]{0,1:T(4,128)S(1)}, s32[6,4]{0,1:T(4,128)}, u32[]{:S(2)}) copy-start(s32[6,4]{0,1:T(4,128)} %param.7) | copy-start | bytes 292
  1.4 19.4 %collective-permute-start.2 = (f32[128,384]{0,1:T(8,128)S(1)}, f32[128,384]{0,1:T(8,128)S(1)}, u32[]{:S(2)}, u32[]{:S(2)}) collective-permute-start(f32[128,384]{0,1:T(8,128)S(1)} %bitcast_multiply_fusion.1), channel_id=1, source_target_pairs={{0,392},{8,0},{16,152},{24,272},{32,184},{40,304},{48,424},{56,32}... | collective-permute-start | bytes 589832 | tf_op jit(solution)/shard_map/ppermute | solution.py:29
  5.9 19.0 %collective-permute-start.5 = (f32[384,256]{0,1:T(8,128)S(1)}, f32[384,256]{0,1:T(8,128)S(1)}, u32[]{:S(2)}, u32[]{:S(2)}) collective-permute-start(f32[384,256]{0,1:T(8,128)S(1)} %bitcast_multiply_fusion), channel_id=1, source_target_pairs={{0,64},{64,0},{1,65},{65,1},{2,66},{66,2},{3,67},{67,3},{4,68},{68... | collective-permute-start | bytes 1179656 | tf_op jit(solution)/shard_map/ppermute | solution.py:29
  11.2 25.1 %collective-permute-start.4 = (f32[384,512]{0,1:T(8,128)S(1)}, f32[384,512]{0,1:T(8,128)S(1)}, u32[]{:S(2)}, u32[]{:S(2)}) collective-permute-start(f32[384,512]{0,1:T(8,128)S(1)} %all_gather.6), channel_id=1, source_target_pairs={{0,8},{8,0},{16,24},{24,16},{32,56},{40,48},{48,40},{56,32},{1,9},... | collective-permute-start | bytes 2359304 | tf_op jit(solution)/shard_map/ppermute | solution.py:29
  13.3 21.2 %collective-permute-start.3 = (f32[128,384]{0,1:T(8,128)S(1)}, f32[128,384]{0,1:T(8,128)S(1)}, u32[]{:S(2)}, u32[]{:S(2)}) collective-permute-start(f32[128,384]{0,1:T(8,128)S(1)} %bitcast_multiply_fusion.1), channel_id=1, source_target_pairs={{0,264},{8,128},{16,24},{24,400},{32,312},{40,176},{48,40},{56,416... | collective-permute-start | bytes 589832 | tf_op jit(solution)/shard_map/ppermute | solution.py:29
  20.1 14.3 %collective-permute-start = (f32[128,384]{0,1:T(8,128)S(1)}, f32[128,384]{0,1:T(8,128)S(1)}, u32[]{:S(2)}, u32[]{:S(2)}) collective-permute-start(f32[128,384]{0,1:T(8,128)S(1)} %bitcast_multiply_fusion.1), channel_id=1, source_target_pairs={{0,0},{8,392},{16,272},{24,152},{32,32},{40,424},{48,304},{56,184}... | collective-permute-start | bytes 589832 | tf_op jit(solution)/shard_map/ppermute | solution.py:29
  20.8 15.5 %collective-permute-start.1 = (f32[128,384]{0,1:T(8,128)S(1)}, f32[128,384]{0,1:T(8,128)S(1)}, u32[]{:S(2)}, u32[]{:S(2)}) collective-permute-start(f32[128,384]{0,1:T(8,128)S(1)} %bitcast_multiply_fusion.1), channel_id=1, source_target_pairs={{0,128},{8,264},{16,400},{24,24},{32,416},{40,40},{48,176},{56,312... | collective-permute-start | bytes 589832 | tf_op jit(solution)/shard_map/ppermute | solution.py:29
  27.2 17.1 %collective-permute-start.6 = (f32[384,512]{0,1:T(8,128)S(1)}, f32[384,512]{0,1:T(8,128)S(1)}, u32[]{:S(2)}, u32[]{:S(2)}) collective-permute-start(f32[384,512]{0,1:T(8,128)S(1)} %all_gather.7), channel_id=1, source_target_pairs={{0,8},{8,0},{16,24},{24,16},{32,56},{40,48},{48,40},{56,32},{1,9},... | collective-permute-start | bytes 2359304 | tf_op jit(solution)/shard_map/ppermute | solution.py:29
  38.1 0.8 copy-start
  46.1 1.0 slice-start
  47.1 12.5 %copy-start.1 = (f32[256,512]{1,0:T(8,128)S(1)}, f32[256,512]{1,0:T(8,128)}, u32[]{:S(2)}) copy-start(f32[256,512]{1,0:T(8,128)} %copy-done) | copy-start | bytes 1572868
  47.1 12.4 %collective-permute-start.7 = (f32[128,1024]{1,0:T(8,128)S(1)}, f32[128,1024]{1,0:T(8,128)S(1)}, u32[]{:S(2)}, u32[]{:S(2)}) collective-permute-start(f32[128,1024]{1,0:T(8,128)S(1)} %pad_maximum_fusion), channel_id=1, source_target_pairs={{0,24},{8,16},{16,8},{24,0},{32,40},{40,32},{48,56},{56,48},{1,25}... | collective-permute-start | bytes 1572872 | tf_op jit(solution)/shard_map/ppermute | solution.py:29
  83.0 13.2 %collective-permute-start.8 = (f32[128,128]{1,0:T(8,128)S(1)}, f32[128,128]{1,0:T(8,128)S(1)}, u32[]{:S(2)}, u32[]{:S(2)}) collective-permute-start(f32[128,128]{1,0:T(8,128)S(1)} %reduce_sum.9), channel_id=1, source_target_pairs={{0,0},{8,128},{16,256},{24,384},{128,136},{136,264},{144,392},{152... | collective-permute-start | bytes 196616 | tf_op jit(solution)/shard_map/ppermute | solution.py:29
where the time goes:
time: 97.3 us; the launch traced here: 96.9 us
  starting transfers between devices  35.9 us (37%)
  blocking collectives  28.6 us (29%)
  waiting for transfers between devices  24.2 us (25%)
  local copies, waits for them, and re-layouts  4.11 us (4%)
  matrix products  3.49 us (4%)
    ppermute x9, starting transfers between devices, send(): return lax.ppermute(value, names, moves(names, target))  35.9 us
    ppermute x9, waiting for transfers between devices, send(): return lax.ppermute(value, names, moves(names, target))  24.2 us
    all_to_all x1, blocking collectives, body(): lax.all_to_all(pieces, AXES, 0, 0, tiled=True, axis_index_groups=groups)  23.2 us
    dot_general x4, matrix products, product(): jnp.dot(a, b, precision=lax.Precision.HIGH, preferred_element_type=jnp.fl...  3.49 us
    all_gather x1, blocking collectives, body(): near = lax.all_gather(masked_v, 'c', axis=1, tiled=True)  2.99 us
    unnamed x15, local copies, waits for them, and re-layouts  2.73 us
    all_gather x1, blocking collectives, body(): far = lax.all_gather(far_half, 'c', axis=1, tiled=True)  2.37 us
  transfers between devices with their start and end apart: 9, of which 4 were waited for; matrix products, arithmetic and copies ran while one was open for 2% of the time, Pallas kernels for 0%

commit v1 on v0

--- a/solution.py
+++ b/solution.py
@@ -5,6 +5,13 @@
 
 AXES = ("h", "l", "c", "x", "z")
 SIZES = (4, 2, 2, 4, 8)
+
+
+def group_marks(x_local):
+    mixed_arr = lax.all_to_all(
+        jnp.stack(tuple((x_local for _ in range(lax.axis_size("c")))), axis=0), "c", 0, 0
+    )
+    return jnp.concatenate(mixed_arr, 1)
 
 
 def moves(names, target):
@@ -47,7 +54,7 @@
     width = amplitudes.shape[1] // pair_mask.shape[1]
     masked_v = integrals * expand(tile_mask, width)
     far_half = send(masked_v, ("l",), lambda at: {"l": at["l"] + 1})
-    near = lax.all_gather(masked_v, "c", axis=1, tiled=True)
+    near = group_marks(masked_v)
     near_beside = send(near, ("c", "x"), lambda at: {"x": at["x"] + sign(at)})
     masked_t = amplitudes * expand(pair_mask, width)
     names = ("h", "c", "x")

time: 97.3 us -> 99.5 us (1.023)
  blocking collectives: 28.6 us -> 30.5 us
    all_to_all x0 -> x1, blocking collectives: none -> 4.86 us  [group_marks(): lax.all_to_all(jnp.stack(tuple((x_local for _ in range(lax.axis_size('c')...]
    all_gather x1 -> x0, blocking collectives: 2.99 us -> none  [body(): near = lax.all_gather(masked_v, 'c', axis=1, tiled=True)]
where the time goes in v1:
time: 99.5 us; the launch traced here: 99.1 us
  starting transfers between devices  36.1 us (36%)
  blocking collectives  30.5 us (31%)
  waiting for transfers between devices  24.1 us (24%)
  local copies, waits for them, and re-layouts  4.14 us (4%)
  matrix products  3.48 us (3%)
    ppermute x9, starting transfers between devices, send(): return lax.ppermute(value, names, moves(names, target))  36.1 us
    ppermute x9, waiting for transfers between devices, send(): return lax.ppermute(value, names, moves(names, target))  24.1 us
    all_to_all x1, blocking collectives, body(): lax.all_to_all(pieces, AXES, 0, 0, tiled=True, axis_index_groups=groups)  23.2 us
    all_to_all x1, blocking collectives, group_marks(): lax.all_to_all(jnp.stack(tuple((x_local for _ in range(lax.axis_size('c')...  4.86 us
    dot_general x4, matrix products, product(): jnp.dot(a, b, precision=lax.Precision.HIGH, preferred_element_type=jnp.fl...  3.48 us
    unnamed x15, local copies, waits for them, and re-layouts  2.75 us
    all_gather x1, blocking collectives, body(): far = lax.all_gather(far_half, 'c', axis=1, tiled=True)  2.46 us
  transfers between devices with their start and end apart: 9, of which 4 were waited for; matrix products, arithmetic and copies ran while one was open for 2% of the time, Pallas kernels for 0%

profile of v1, /device:TPU:40, one launch (start us, length us, event | category | flops | bytes accessed | tf_op | source)
XLA Modules:
  0.0 99.1 jit_solution(8597249875948697194)
XLA Ops:
  0.0 1.2 %copy.14 = f32[384,256]{0,1:T(8,128)S(1)} copy(f32[384,256]{1,0:T(8,128)} %param.5) | data formatting | bytes 786432 | tf_op args[1]
  1.2 0.1 broadcast_in_dim.14
  1.3 0.1 reshape.23
  1.4 3.4 %collective-permute-start.5 = (f32[384,256]{0,1:T(8,128)S(1)}, f32[384,256]{0,1:T(8,128)S(1)}, u32[]{:S(2)}, u32[]{:S(2)}) collective-permute-start(f32[384,256]{0,1:T(8,128)S(1)} %bitcast_multiply_fusion), channel_id=1, source_target_pairs={{0,64},{64,0},{1,65},{65,1},{2,66},{66,2},{3,67},{67,3},{4,68},{68... | collective-permute-start | bytes 1179656 | tf_op jit(solution)/shard_map/ppermute | solution.py:36
  4.8 0.1 copy.13
  5.0 0.1 copy.12
  5.1 0.1 broadcast_in_dim.12
  5.1 0.1 reshape.21
  5.2 3.2 %collective-permute-start.2 = (f32[128,384]{0,1:T(8,128)S(1)}, f32[128,384]{0,1:T(8,128)S(1)}, u32[]{:S(2)}, u32[]{:S(2)}) collective-permute-start(f32[128,384]{0,1:T(8,128)S(1)} %bitcast_multiply_fusion.1), channel_id=1, source_target_pairs={{0,392},{8,0},{16,152},{24,272},{32,184},{40,304},{48,424},{56,32}... | collective-permute-start | bytes 589832 | tf_op jit(solution)/shard_map/ppermute | solution.py:36
  8.5 4.9 %all_to_all.10 = f32[2,384,256]{1,2,0:T(8,128)S(1)} all-to-all(f32[2,384,256]{1,2,0:T(8,128)S(1)} %pad_maximum_fusion), channel_id=1, replica_groups=mesh['h'=4,'l'=2,'c'=2,'x'=4,'z'=8] {'c'}, dimensions={0} | all-to-all | bytes 1572864 | tf_op jit(solution)/shard_map/all_to_all | solution.py:11
  13.3 2.2 %collective-permute-start.4 = (f32[384,512]{0,1:T(8,128)S(1)}, f32[384,512]{0,1:T(8,128)S(1)}, u32[]{:S(2)}, u32[]{:S(2)}) collective-permute-start(f32[384,512]{0,1:T(8,128)S(1)} %bitcast.27), channel_id=1, source_target_pairs={{0,8},{8,0},{16,24},{24,16},{32,56},{40,48},{48,40},{56,32},{1,9},... | collective-permute-start | bytes 2359304 | tf_op jit(solution)/shard_map/ppermute | solution.py:36
  15.5 6.8 %collective-permute-start.3 = (f32[128,384]{0,1:T(8,128)S(1)}, f32[128,384]{0,1:T(8,128)S(1)}, u32[]{:S(2)}, u32[]{:S(2)}) collective-permute-start(f32[128,384]{0,1:T(8,128)S(1)} %bitcast_multiply_fusion.1), channel_id=1, source_target_pairs={{0,264},{8,128},{16,24},{24,400},{32,312},{40,176},{48,40},{56,416... | collective-permute-start | bytes 589832 | tf_op jit(solution)/shard_map/ppermute | solution.py:36
  22.4 0.7 collective-permute-start
  23.0 3.9 %collective-permute-start.1 = (f32[128,384]{0,1:T(8,128)S(1)}, f32[128,384]{0,1:T(8,128)S(1)}, u32[]{:S(2)}, u32[]{:S(2)}) collective-permute-start(f32[128,384]{0,1:T(8,128)S(1)} %bitcast_multiply_fusion.1), channel_id=1, source_target_pairs={{0,128},{8,264},{16,400},{24,24},{32,416},{40,40},{48,176},{56,312... | collective-permute-start | bytes 589832 | tf_op jit(solution)/shard_map/ppermute | solution.py:36
  27.0 2.5 %all_gather.3 = f32[384,512]{0,1:T(8,128)S(1)} all-gather(f32[384,256]{0,1:T(8,128)S(1)} %collective-permute-done.5), channel_id=1, replica_groups=mesh['h'=4,'l'=2,'c'=2,'x'=4,'z'=8] {'c'}, dimensions={1}, use_global_device_ids=true | all-gather | bytes 1179648 | tf_op jit(solution)/shard_map/all_gather | solution.py:81
  29.4 7.2 %collective-permute-start.6 = (f32[384,512]{0,1:T(8,128)S(1)}, f32[384,512]{0,1:T(8,128)S(1)}, u32[]{:S(2)}, u32[]{:S(2)}) collective-permute-start(f32[384,512]{0,1:T(8,128)S(1)} %all_gather.3), channel_id=1, source_target_pairs={{0,8},{8,0},{16,24},{24,16},{32,56},{40,48},{48,40},{56,32},{1,9},... | collective-permute-start | bytes 2359304 | tf_op jit(solution)/shard_map/ppermute | solution.py:36
  36.7 1.8 %collective-permute-done.1 = f32[128,384]{0,1:T(8,128)S(1)} collective-permute-done((f32[128,384]{0,1:T(8,128)S(1)}, f32[128,384]{0,1:T(8,128)S(1)}, u32[]{:S(2)}, u32[]{:S(2)}) %collective-permute-start.1) | collective-permute-done | bytes 196640 | tf_op jit(solution)/shard_map/ppermute | solution.py:36
  38.6 0.9 fusion.1
  39.5 0.9 convolution_add_fusion.1
  40.4 0.8 copy-done
  41.1 5.5 %collective-permute-done.6 = f32[384,512]{0,1:T(8,128)S(1)} collective-permute-done((f32[384,512]{0,1:T(8,128)S(1)}, f32[384,512]{0,1:T(8,128)S(1)}, u32[]{:S(2)}, u32[]{:S(2)}) %collective-permute-start.6) | collective-permute-done | bytes 786464 | tf_op jit(solution)/shard_map/ppermute | solution.py:36
  46.6 0.9 fusion.2
  47.5 0.9 convolution_add_fusion
  48.4 0.9 slice-done
  49.3 4.2 %collective-permute-start.7 = (f32[128,1024]{1,0:T(8,128)S(1)}, f32[128,1024]{1,0:T(8,128)S(1)}, u32[]{:S(2)}, u32[]{:S(2)}) collective-permute-start(f32[128,1024]{1,0:T(8,128)S(1)} %pad_maximum_fusion.1), channel_id=1, source_target_pairs={{0,24},{8,16},{16,8},{24,0},{32,40},{40,32},{48,56},{56,48},{1,25}... | collective-permute-start | bytes 1572872 | tf_op jit(solution)/shard_map/ppermute | solution.py:36
  53.5 8.3 %collective-permute-done.7 = f32[128,1024]{1,0:T(8,128)S(1)} collective-permute-done((f32[128,1024]{1,0:T(8,128)S(1)}, f32[128,1024]{1,0:T(8,128)S(1)}, u32[]{:S(2)}, u32[]{:S(2)}) %collective-permute-start.7) | collective-permute-done | bytes 524320 | tf_op jit(solution)/shard_map/ppermute | solution.py:36
  61.8 0.1 broadcast_select_fusion.1
  61.9 0.1 fusion
  62.0 23.2 %all_to_all.11 = f32[8,128,128]{2,1,0:T(8,128)S(1)} all-to-all(f32[8,128,128]{2,1,0:T(8,128)S(1)} %fusion), channel_id=1, replica_groups={{0,1,2,3,4,5,6,7},{8,9,10,11,12,13,14,15},{16,17,18,19,20,21,22,23},{24..., dimensions={0} | all-to-all | bytes 1048576 | tf_op jit(solution)/shard_map/all_to_all | solution.py:100
  85.3 4.6 %collective-permute-start.8 = (f32[128,128]{1,0:T(8,128)S(1)}, f32[128,128]{1,0:T(8,128)S(1)}, u32[]{:S(2)}, u32[]{:S(2)}) collective-permute-start(f32[128,128]{1,0:T(8,128)S(1)} %reduce_sum.9), channel_id=1, source_target_pairs={{0,0},{8,128},{16,256},{24,384},{128,136},{136,264},{144,392},{152... | collective-permute-start | bytes 196616 | tf_op jit(solution)/shard_map/ppermute | solution.py:36
  89.9 8.6 %collective-permute-done.8 = f32[128,128]{1,0:T(8,128)S(1)} collective-permute-done((f32[128,128]{1,0:T(8,128)S(1)}, f32[128,128]{1,0:T(8,128)S(1)}, u32[]{:S(2)}, u32[]{:S(2)}) %collective-permute-start.8) | collective-permute-done | bytes 65568 | tf_op jit(solution)/shard_map/ppermute | solution.py:36
  98.4 0.6 copy.21
  (29 shorter events, 0.3 us)
Async XLA Ops:
  0.0 1.2 %copy-start.3 = (s32[6,4]{0,1:T(4,128)S(1)}, s32[6,4]{0,1:T(4,128)}, u32[]{:S(2)}) copy-start(s32[6,4]{0,1:T(4,128)} %param.7) | copy-start | bytes 292
  1.4 3.4 %copy-start.2 = (f32[128,384]{1,0:T(8,128)S(1)}, f32[128,384]{1,0:T(8,128)}, u32[]{:S(2)}) copy-start(f32[128,384]{1,0:T(8,128)} %param.4) | copy-start | bytes 589828
  1.4 3.5 %copy-start.4 = (s32[2,6]{1,0:T(2,128)S(1)}, s32[2,6]{1,0:T(2,128)}, u32[]{:S(2)}) copy-start(s32[2,6]{1,0:T(2,128)} %param.6) | copy-start | bytes 148
  1.4 25.6 %collective-permute-start.5 = (f32[384,256]{0,1:T(8,128)S(1)}, f32[384,256]{0,1:T(8,128)S(1)}, u32[]{:S(2)}, u32[]{:S(2)}) collective-permute-start(f32[384,256]{0,1:T(8,128)S(1)} %bitcast_multiply_fusion), channel_id=1, source_target_pairs={{0,64},{64,0},{1,65},{65,1},{2,66},{66,2},{3,67},{67,3},{4,68},{68... | collective-permute-start | bytes 1179656 | tf_op jit(solution)/shard_map/ppermute | solution.py:36
  5.2 17.8 %collective-permute-start.2 = (f32[128,384]{0,1:T(8,128)S(1)}, f32[128,384]{0,1:T(8,128)S(1)}, u32[]{:S(2)}, u32[]{:S(2)}) collective-permute-start(f32[128,384]{0,1:T(8,128)S(1)} %bitcast_multiply_fusion.1), channel_id=1, source_target_pairs={{0,392},{8,0},{16,152},{24,272},{32,184},{40,304},{48,424},{56,32}... | collective-permute-start | bytes 589832 | tf_op jit(solution)/shard_map/ppermute | solution.py:36
  13.3 25.2 %collective-permute-start.4 = (f32[384,512]{0,1:T(8,128)S(1)}, f32[384,512]{0,1:T(8,128)S(1)}, u32[]{:S(2)}, u32[]{:S(2)}) collective-permute-start(f32[384,512]{0,1:T(8,128)S(1)} %bitcast.27), channel_id=1, source_target_pairs={{0,8},{8,0},{16,24},{24,16},{32,56},{40,48},{48,40},{56,32},{1,9},... | collective-permute-start | bytes 2359304 | tf_op jit(solution)/shard_map/ppermute | solution.py:36
  15.5 21.2 %collective-permute-start.3 = (f32[128,384]{0,1:T(8,128)S(1)}, f32[128,384]{0,1:T(8,128)S(1)}, u32[]{:S(2)}, u32[]{:S(2)}) collective-permute-start(f32[128,384]{0,1:T(8,128)S(1)} %bitcast_multiply_fusion.1), channel_id=1, source_target_pairs={{0,264},{8,128},{16,24},{24,400},{32,312},{40,176},{48,40},{56,416... | collective-permute-start | bytes 589832 | tf_op jit(solution)/shard_map/ppermute | solution.py:36
  22.4 14.3 %collective-permute-start = (f32[128,384]{0,1:T(8,128)S(1)}, f32[128,384]{0,1:T(8,128)S(1)}, u32[]{:S(2)}, u32[]{:S(2)}) collective-permute-start(f32[128,384]{0,1:T(8,128)S(1)} %bitcast_multiply_fusion.1), channel_id=1, source_target_pairs={{0,0},{8,392},{16,272},{24,152},{32,32},{40,424},{48,304},{56,184}... | collective-permute-start | bytes 589832 | tf_op jit(solution)/shard_map/ppermute | solution.py:36
  23.0 15.5 %collective-permute-start.1 = (f32[128,384]{0,1:T(8,128)S(1)}, f32[128,384]{0,1:T(8,128)S(1)}, u32[]{:S(2)}, u32[]{:S(2)}) collective-permute-start(f32[128,384]{0,1:T(8,128)S(1)} %bitcast_multiply_fusion.1), channel_id=1, source_target_pairs={{0,128},{8,264},{16,400},{24,24},{32,416},{40,40},{48,176},{56,312... | collective-permute-start | bytes 589832 | tf_op jit(solution)/shard_map/ppermute | solution.py:36
  29.4 17.2 %collective-permute-start.6 = (f32[384,512]{0,1:T(8,128)S(1)}, f32[384,512]{0,1:T(8,128)S(1)}, u32[]{:S(2)}, u32[]{:S(2)}) collective-permute-start(f32[384,512]{0,1:T(8,128)S(1)} %all_gather.3), channel_id=1, source_target_pairs={{0,8},{8,0},{16,24},{24,16},{32,56},{40,48},{48,40},{56,32},{1,9},... | collective-permute-start | bytes 2359304 | tf_op jit(solution)/shard_map/ppermute | solution.py:36
  40.4 0.8 copy-start
  48.4 1.0 slice-start
  49.3 12.5 %copy-start.1 = (f32[256,512]{1,0:T(8,128)S(1)}, f32[256,512]{1,0:T(8,128)}, u32[]{:S(2)}) copy-start(f32[256,512]{1,0:T(8,128)} %copy-done) | copy-start | bytes 1572868
  49.3 12.4 %collective-permute-start.7 = (f32[128,1024]{1,0:T(8,128)S(1)}, f32[128,1024]{1,0:T(8,128)S(1)}, u32[]{:S(2)}, u32[]{:S(2)}) collective-permute-start(f32[128,1024]{1,0:T(8,128)S(1)} %pad_maximum_fusion.1), channel_id=1, source_target_pairs={{0,24},{8,16},{16,8},{24,0},{32,40},{40,32},{48,56},{56,48},{1,25}... | collective-permute-start | bytes 1572872 | tf_op jit(solution)/shard_map/ppermute | solution.py:36
  85.3 13.2 %collective-permute-start.8 = (f32[128,128]{1,0:T(8,128)S(1)}, f32[128,128]{1,0:T(8,128)S(1)}, u32[]{:S(2)}, u32[]{:S(2)}) collective-permute-start(f32[128,128]{1,0:T(8,128)S(1)} %reduce_sum.9), channel_id=1, source_target_pairs={{0,0},{8,128},{16,256},{24,384},{128,136},{136,264},{144,392},{152... | collective-permute-start | bytes 196616 | tf_op jit(solution)/shard_map/ppermute | solution.py:36
